TPU v7x, 32 devices: a whole 2x2x4 slice. The times are simulated.
32 devices in a mesh: ctx: 16 (over z, x, core), head: 2 (over y).
Axes of the slice: x: 2, y: 2, z: 4, core: 2. Of those that a mesh axis runs over, the one named last changes fastest.
Arguments:
- queries: bfloat16 [6144, 2048], P('ctx', 'head')
- keys: bfloat16 [6144, 512], P('ctx', 'head')
- values: bfloat16 [6144, 512], P('ctx', 'head'), may hold values from -6 to 6
- block_start: int32 [48], P('ctx'), may hold values from 0 to 6016, as said below
- out_weight: bfloat16 [2048, 4096], P('head'), may hold values from -0.125 to 0.125
Outputs:
- attended: bfloat16 [6144, 4096], P('ctx', 'head')
Inputs may be any that keep to these rules, and one draw needn't show every extreme that they name: block_start never falls; every document is a whole number of blocks and at most 3072 tokens long, and one document is exactly 3072 tokens long; the first and the last block each begin a document.
All inputs are finite; a program needn't handle non-finite values.
Results may differ from a plain program's by a relative error of at most 0.012.
Values may be sent and summed in bfloat16 or wider, within the bound.
No kernel may reach another device: no remote copies, remote signals or barrier semaphores. Data moves between devices by JAX's collectives and lax.ppermute only.
A program may use at most 64 MiB of HBM per device.

v0:
```python
import jax
import jax.numpy as jnp
from jax import lax
from jax.sharding import PartitionSpec as P

HEAD_SIZE = 128
BLOCK = 128
SPAN = 8


def from_behind(block, axis, distance):
    devices = range(lax.axis_size(axis))
    route = [(i - distance, i) for i in devices if i - distance in devices]
    return lax.ppermute(block, axis, route)


def per_device(queries, keys, values, block_start, out_weight):
    tok = queries.shape[0]
    kv_heads = keys.shape[1] // HEAD_SIZE
    q_heads = queries.shape[1] // HEAD_SIZE
    query_group = q_heads // kv_heads
    scale = HEAD_SIZE ** (-0.5)
    first_token = lax.axis_index("ctx") * tok
    q_pos = first_token + jnp.arange(tok, dtype=jnp.int32)
    starts = jnp.repeat(block_start, BLOCK)
    lowest = jnp.min(starts)
    query_rows = queries.reshape(tok, kv_heads, query_group, HEAD_SIZE)
    packed = jnp.stack([keys, values])

    def attend(state, pair, key_first):
        top, total, accum = state
        key_blk = pair[0].reshape(tok, kv_heads, HEAD_SIZE)
        val_blk = pair[1].reshape(tok, kv_heads, HEAD_SIZE)
        scores = (
            jnp.einsum("pgcd,jgd->gcpj", query_rows, key_blk, preferred_element_type=jnp.float32)
            * scale
        )
        k_pos = key_first + jnp.arange(tok, dtype=jnp.int32)
        valid = (k_pos[None, :] >= starts[:, None]) & (k_pos[None, :] <= q_pos[:, None])
        masked = jnp.where(valid, scores, -1e30)
        top_new = jnp.maximum(top, jnp.max(masked, axis=-1))
        factor = jnp.exp(top - top_new)
        expw = jnp.where(valid, jnp.exp(masked - top_new[..., None]), 0.0)
        total = total * factor + jnp.sum(expw, axis=-1)
        update = jnp.einsum(
            "gcpj,jgd->gcpd", expw.astype(jnp.bfloat16), val_blk, preferred_element_type=jnp.float32
        )
        accum = accum * factor[..., None] + update
        return (top_new, total, accum)

    state = (
        jnp.full((kv_heads, query_group, tok), -1e30, jnp.float32),
        jnp.zeros((kv_heads, query_group, tok), jnp.float32),
        jnp.zeros((kv_heads, query_group, tok, HEAD_SIZE), jnp.float32),
    )
    state = attend(state, packed, first_token)
    moving = packed
    for step in range(1, SPAN + 1):
        moving = from_behind(moving, "ctx", 1)
        maybe_pair = moving
        maybe_key_first = first_token - step * tok
        needed = lowest <= maybe_key_first + tok - 1
        state = lax.cond(
            needed, lambda s: attend(s, maybe_pair, maybe_key_first), lambda s: s, state
        )
    top, total, accum = state
    heads_out = (accum / total[..., None]).astype(jnp.bfloat16)
    heads_out = jnp.transpose(heads_out, (2, 0, 1, 3)).reshape(tok, q_heads * HEAD_SIZE)
    summed = lax.psum_scatter(
        lax.dot_general(
            out_weight, heads_out, (((0,), (1,)), ((), ())), preferred_element_type=jnp.float32
        ).astype(jnp.bfloat16),
        "head",
        scatter_dimension=0,
        tiled=True,
    ).astype(jnp.float32)
    return summed.T.astype(jnp.bfloat16)


def solution(mesh):
    in_specs = (P("ctx", "head"), P("ctx", "head"), P("ctx", "head"), P("ctx"), P("head", None))
    out_specs = P("ctx", "head")
    return jax.shard_map(
        per_device, mesh=mesh, in_specs=in_specs, out_specs=out_specs, check_vma=False
    )
```

profile of v0, /device:TPU:2, one launch (start us, length us, event | category | flops | bytes accessed | tf_op | source)
XLA Modules:
  0.0 180.7 jit_solution(15667862274945219988)
XLA Ops:
  6.5 0.0 reduce-scatter.2.cloned.1.call-start
  6.5 1.1 copy.46
  7.6 1.1 copy.47
  8.8 1.9 %collective-permute-start = (bf16[2,384,256]{1,2,0:T(8,128)(2,1)S(1)}, bf16[2,384,256]{1,2,0:T(8,128)(2,1)S(1)}, u32[]{:S(2)}, u32[]{:S(2)}) collective-permute-start(bf16[2,384,256]{1,2,0:T(8,128)(2,1)S(1)} %pad_maximum_fusion), channel_id=1, source_target_pairs={{0,2},{2,4},{4,6},{6,8},{8,10},{10,12},{12,14},{14,16},{16,18},{18... | collective-permute-start | bytes 1179656 | tf_op jit(solution)/shard_map/ppermute | solution.py:14
  10.7 7.2 %collective-permute-done = bf16[2,384,256]{1,2,0:T(8,128)(2,1)S(1)} collective-permute-done((bf16[2,384,256]{1,2,0:T(8,128)(2,1)S(1)}, bf16[2,384,256]{1,2,0:T(8,128)(2,1)S(1)}, u32[]{:S(2)}, u32[]{:S(2)}) %collective-permute-start) | collective-permute-done | bytes 393248 | tf_op jit(solution)/shard_map/ppermute | solution.py:14
  17.9 0.0 copy-start.10
  17.9 1.9 %collective-permute-start.1 = (bf16[2,384,256]{1,2,0:T(8,128)(2,1)S(1)}, bf16[2,384,256]{1,2,0:T(8,128)(2,1)S(1)}, u32[]{:S(2)}, u32[]{:S(2)}) collective-permute-start(bf16[2,384,256]{1,2,0:T(8,128)(2,1)S(1)} %collective-permute-done), channel_id=1, source_target_pairs={{0,2},{2,4},{4,6},{6,8},{8,10},{10,12},{12,14},{14,16},{16,18},{18... | collective-permute-start | bytes 1179656 | tf_op jit(solution)/shard_map/ppermute | solution.py:14
  19.8 0.0 copy-done.10
  19.8 7.2 %collective-permute-done.1 = bf16[2,384,256]{1,2,0:T(8,128)(2,1)S(1)} collective-permute-done((bf16[2,384,256]{1,2,0:T(8,128)(2,1)S(1)}, bf16[2,384,256]{1,2,0:T(8,128)(2,1)S(1)}, u32[]{:S(2)}, u32[]{:S(2)}) %collective-permute-start.1) | collective-permute-done | bytes 393248 | tf_op jit(solution)/shard_map/ppermute | solution.py:14
  27.0 0.0 copy-start.8
  27.0 2.0 %collective-permute-start.2 = (bf16[2,384,256]{1,2,0:T(8,128)(2,1)S(1)}, bf16[2,384,256]{1,2,0:T(8,128)(2,1)S(1)}, u32[]{:S(2)}, u32[]{:S(2)}) collective-permute-start(bf16[2,384,256]{1,2,0:T(8,128)(2,1)S(1)} %collective-permute-done.1), channel_id=1, source_target_pairs={{0,2},{2,4},{4,6},{6,8},{8,10},{10,12},{12,14},{14,16},{16,18},{18... | collective-permute-start | bytes 1179656 | tf_op jit(solution)/shard_map/ppermute | solution.py:14
  28.9 7.1 %collective-permute-done.2 = bf16[2,384,256]{1,2,0:T(8,128)(2,1)S(1)} collective-permute-done((bf16[2,384,256]{1,2,0:T(8,128)(2,1)S(1)}, bf16[2,384,256]{1,2,0:T(8,128)(2,1)S(1)}, u32[]{:S(2)}, u32[]{:S(2)}) %collective-permute-start.2) | collective-permute-done | bytes 393248 | tf_op jit(solution)/shard_map/ppermute | solution.py:14
  36.1 2.9 %collective-permute-start.3 = (bf16[2,384,256]{1,2,0:T(8,128)(2,1)S(1)}, bf16[2,384,256]{1,2,0:T(8,128)(2,1)S(1)}, u32[]{:S(2)}, u32[]{:S(2)}) collective-permute-start(bf16[2,384,256]{1,2,0:T(8,128)(2,1)S(1)} %collective-permute-done.2), channel_id=1, source_target_pairs={{0,2},{2,4},{4,6},{6,8},{8,10},{10,12},{12,14},{14,16},{16,18},{18... | collective-permute-start | bytes 1179656 | tf_op jit(solution)/shard_map/ppermute | solution.py:14
  38.9 6.2 %collective-permute-done.3 = bf16[2,384,256]{1,2,0:T(8,128)(2,1)S(1)} collective-permute-done((bf16[2,384,256]{1,2,0:T(8,128)(2,1)S(1)}, bf16[2,384,256]{1,2,0:T(8,128)(2,1)S(1)}, u32[]{:S(2)}, u32[]{:S(2)}) %collective-permute-start.3) | collective-permute-done | bytes 393248 | tf_op jit(solution)/shard_map/ppermute | solution.py:14
  45.1 0.0 copy-done.8
  45.1 0.0 copy-done.7
  45.1 3.8 %collective-permute-start.4 = (bf16[2,384,256]{1,2,0:T(8,128)(2,1)S(1)}, bf16[2,384,256]{1,2,0:T(8,128)(2,1)S(1)}, u32[]{:S(2)}, u32[]{:S(2)}) collective-permute-start(bf16[2,384,256]{1,2,0:T(8,128)(2,1)S(1)} %collective-permute-done.3), channel_id=1, source_target_pairs={{0,2},{2,4},{4,6},{6,8},{8,10},{10,12},{12,14},{14,16},{16,18},{18... | collective-permute-start | bytes 1179656 | tf_op jit(solution)/shard_map/ppermute | solution.py:14
  48.9 1.4 broadcast_bitcast_fusion
  50.3 1.0 reshape_squeeze_stack.6
  51.3 1.5 copy.41
  52.8 0.2 compare_and_fusion.8
  53.0 0.0 copy-done.5
  53.0 1.2 collective-permute-done.4
  54.2 4.7 %collective-permute-start.5 = (bf16[2,384,256]{1,2,0:T(8,128)(2,1)S(1)}, bf16[2,384,256]{1,2,0:T(8,128)(2,1)S(1)}, u32[]{:S(2)}, u32[]{:S(2)}) collective-permute-start(bf16[2,384,256]{1,2,0:T(8,128)(2,1)S(1)} %collective-permute-done.4), channel_id=1, source_target_pairs={{0,2},{2,4},{4,6},{6,8},{8,10},{10,12},{12,14},{14,16},{16,18},{18... | collective-permute-start | bytes 1179656 | tf_op jit(solution)/shard_map/ppermute | solution.py:14
  58.9 0.0 copy-start.1
  58.9 0.9 fusion.89
  59.9 0.0 copy-start
  59.9 3.4 %collective-permute-done.5 = bf16[2,384,256]{1,2,0:T(8,128)(2,1)S(1)} collective-permute-done((bf16[2,384,256]{1,2,0:T(8,128)(2,1)S(1)}, bf16[2,384,256]{1,2,0:T(8,128)(2,1)S(1)}, u32[]{:S(2)}, u32[]{:S(2)}) %collective-permute-start.5) | collective-permute-done | bytes 393248 | tf_op jit(solution)/shard_map/ppermute | solution.py:14
  63.3 5.6 %collective-permute-start.6 = (bf16[2,384,256]{1,2,0:T(8,128)(2,1)S(1)}, bf16[2,384,256]{1,2,0:T(8,128)(2,1)}, u32[]{:S(2)}, u32[]{:S(2)}) collective-permute-start(bf16[2,384,256]{1,2,0:T(8,128)(2,1)S(1)} %collective-permute-done.5), channel_id=1, source_target_pairs={{0,2},{2,4},{4,6},{6,8},{8,10},{10,12},{12,14},{14,16},{16,18},{18... | collective-permute-start | bytes 1179656 | tf_op jit(solution)/shard_map/ppermute | solution.py:14
  68.9 0.0 copy-done
  68.9 1.2 fusion.91
  70.1 0.0 copy-done.1
  70.1 0.1 reshape_squeeze_stack.7
  75.1 0.0 collective-permute-done.6
  75.1 5.3 %collective-permute-start.7 = (bf16[2,384,256]{1,2,0:T(8,128)(2,1)}, bf16[2,384,256]{1,2,0:T(8,128)(2,1)S(1)}, u32[]{:S(2)}, u32[]{:S(2)}) collective-permute-start(bf16[2,384,256]{1,2,0:T(8,128)(2,1)} %collective-permute-done.6), channel_id=1, source_target_pairs={{0,2},{2,4},{4,6},{6,8},{8,10},{10,12},{12,14},{14,16},{16,18},{18... | collective-permute-start | bytes 1179656 | tf_op jit(solution)/shard_map/ppermute | solution.py:14
  80.4 0.0 copy-done.4
  80.4 0.0 copy-done.2
  80.4 0.0 copy-start.11
  80.4 3.6 %fusion.95 = f32[2,4,384,128]{3,2,1,0:T(8,128)S(1)} fusion(f32[2,384,384,4]{2,1,3,0:T(8,128)} %copy-done, f32[2,4,384]{2,1,0:T(4,128)S(1)} %broadcast_maximum_fusion, pred[384,384]{0,1:T(8,128)(4,1)S(1)} %compare_and_fusion.8, f32[2,4,384]{2,1,0:T(4,128)S(1)} %get-tuple-element.440, bf16[384,2,128,1]{2,1,0,3:T(2,128)(2,1)S(1)} %bitcast.345), kind=kOutput, calls=%fused_computation.130 | convolution fusion | flops 308281344 | bytes 6660096 | tf_op jit(solution)/shard_map/gcpj,jgd->gcpd/dot_general | solution.py:45
  84.0 0.0 copy-done.11
  84.0 0.1 broadcast_in_dim.154
  84.1 5.5 %conditional.8 = ((f32[2,4,384]{2,1,0:T(4,128)S(1)}, f32[2,4,384]{2,1,0:T(4,128)S(1)}, f32[2,4,384,128]{3,2,1,0:T(8,128)S(1)})) conditional(s32[]{:T(128)} %convert_element_type.74, (f32[2,4,384]{2,1,0:T(4,128)S(1)}, f32[2,4,384]{2,1,0:T(4,128)S(1)}, f32[2,4,384,128]{3,2,1,0:T(8,128)S(1)}) %tuple.61, (s32[]{:T(128)}, s32[3,128]{1,0:T(4,128)S(1)}, ...), branch_computations={%region_3.4_spmd, %region_4.7_spmd} | conditional | flops 620550528 | bytes 20060196 | solution.py:63
  84.1 0.2 compare_and_fusion
  84.3 1.1 fusion.105
  85.3 1.0 fusion
  86.3 1.1 fusion.2
  87.5 2.0 %multiply_add_fusion = f32[2,4,384,128]{3,2,1,0:T(8,128)S(1)} fusion(f32[2,4,384,128]{3,2,1,0:T(8,128)S(1)} %get-tuple-element.222, bf16[384,2,128,1]{0,2,3,1:T(8,128)(2,1)S(1)} %bitcast.346, f32[2,384,384,4]{2,1,3,0:T(8,128)S(1)} %get-tuple-element.411, f32[2,4,384]{2,1,0:T(4,128)S(1)} %max.18, pred[384,384]{0,1:T(8,128)(4,1)S(1)} %compare_and_fusion, ...), kind=kOutput, calls=%fused_computation.7 | convolution fusion | flops 308674560 | bytes 8232960 | tf_op jit(solution)/shard_map/cond/branch_1_fun/gcpj,jgd->gcpd/dot_general | solution.py:45
  89.6 0.0 copy-done.9
  89.6 4.5 %conditional.9 = ((f32[2,4,384]{2,1,0:T(4,128)S(1)}, f32[2,4,384]{2,1,0:T(4,128)S(1)}, f32[2,4,384,128]{3,2,1,0:T(8,128)S(1)})) conditional(s32[]{:T(128)} %convert_element_type.73, (f32[2,4,384]{2,1,0:T(4,128)S(1)}, f32[2,4,384]{2,1,0:T(4,128)S(1)}, f32[2,4,384,128]{3,2,1,0:T(8,128)S(1)}) %get-tuple-element.508, (s32[]{:T(128)}, ...), branch_computations={%region_7.8_spmd, %region_8.11_spmd} | conditional | flops 620550528 | bytes 20060196 | solution.py:63
  89.6 0.2 compare_and_fusion.1
  89.8 1.0 fusion.11
  90.8 1.1 fusion.13
  92.0 2.0 %multiply_add_fusion.2 = f32[2,4,384,128]{3,2,1,0:T(8,128)S(1)} fusion(f32[2,4,384,128]{3,2,1,0:T(8,128)S(1)} %get-tuple-element.230, bf16[384,2,128,1]{0,2,3,1:T(8,128)(2,1)S(1)} %bitcast.347, f32[2,384,384,4]{2,1,3,0:T(8,128)S(1)} %get-tuple-element.415, f32[2,4,384]{2,1,0:T(4,128)S(1)} %max.19, pred[384,384]{0,1:T(8,128)(4,1)S(1)} %compare_and_fusion.1, ...), kind=kOutput, calls=%fused_computation.22 | convolution fusion | flops 308674560 | bytes 8232960 | tf_op jit(solution)/shard_map/cond/branch_1_fun/gcpj,jgd->gcpd/dot_general | solution.py:45
  94.1 0.0 copy-start.6
  94.1 0.2 conditional.10
  94.3 0.8 copy-done.6
  95.1 1.0 copy-done.3
  96.1 0.0 collective-permute-done.7
  96.1 0.7 conditional.15
  96.1 0.5 copy.129
  96.8 0.1 divide_convert_fusion
  97.0 8.5 %fusion.88 = bf16[4096,384]{0,1:T(8,128)(2,1)} fusion(bf16[384,1024]{0,1:T(8,128)(2,1)S(1)} %bitcast.337, bf16[1024,4096]{1,0:T(8,128)(2,1)} %param.25), kind=kOutput, calls=%fused_computation.121 | convolution fusion | flops 3222798336 | bytes 12320768 | tf_op jit(solution)/shard_map/dot_general | solution.py:70
  105.5 0.0 reduce-scatter.2.cloned.1.call-update
  105.5 68.3 %reduce-scatter.2.cloned.1.call-done = bf16[2048,384]{0,1:T(8,128)(2,1)} async-done(((bf16[4096,384]{0,1:T(8,128)(2,1)}), bf16[2048,384]{0,1:T(8,128)(2,1)}) %reduce-scatter.2.cloned.1.call-update) | async-done | bytes 1572880 | tf_op jit(solution)/shard_map/reduce_scatter | solution.py:69
  (23 shorter events, 0.2 us)
Async XLA Ops:
  6.5 167.3 %reduce-scatter.2.cloned.1.call-start = ((), (), s32[]{:S(2)}) async-start(), calls=%async_computation.1 | async-start | bytes 4718592 | tf_op jit(solution)/shard_map/reduce_scatter | solution.py:69
  8.8 9.1 %collective-permute-start = (bf16[2,384,256]{1,2,0:T(8,128)(2,1)S(1)}, bf16[2,384,256]{1,2,0:T(8,128)(2,1)S(1)}, u32[]{:S(2)}, u32[]{:S(2)}) collective-permute-start(bf16[2,384,256]{1,2,0:T(8,128)(2,1)S(1)} %pad_maximum_fusion), channel_id=1, source_target_pairs={{0,2},{2,4},{4,6},{6,8},{8,10},{10,12},{12,14},{14,16},{16,18},{18... | collective-permute-start | bytes 1179656 | tf_op jit(solution)/shard_map/ppermute | solution.py:14
  17.9 1.9 %copy-start.10 = (bf16[2,384,256]{1,2,0:T(8,128)(2,1)}, bf16[2,384,256]{1,2,0:T(8,128)(2,1)S(1)}, u32[]{:S(2)}) copy-start(bf16[2,384,256]{1,2,0:T(8,128)(2,1)S(1)} %collective-permute-done) | copy-start | bytes 1179652
  17.9 9.1 %collective-permute-start.1 = (bf16[2,384,256]{1,2,0:T(8,128)(2,1)S(1)}, bf16[2,384,256]{1,2,0:T(8,128)(2,1)S(1)}, u32[]{:S(2)}, u32[]{:S(2)}) collective-permute-start(bf16[2,384,256]{1,2,0:T(8,128)(2,1)S(1)} %collective-permute-done), channel_id=1, source_target_pairs={{0,2},{2,4},{4,6},{6,8},{8,10},{10,12},{12,14},{14,16},{16,18},{18... | collective-permute-start | bytes 1179656 | tf_op jit(solution)/shard_map/ppermute | solution.py:14
  27.0 18.2 %copy-start.8 = (bf16[2,384,256]{1,2,0:T(8,128)(2,1)}, bf16[2,384,256]{1,2,0:T(8,128)(2,1)S(1)}, u32[]{:S(2)}) copy-start(bf16[2,384,256]{1,2,0:T(8,128)(2,1)S(1)} %collective-permute-done.1) | copy-start | bytes 1179652
  27.0 9.1 %collective-permute-start.2 = (bf16[2,384,256]{1,2,0:T(8,128)(2,1)S(1)}, bf16[2,384,256]{1,2,0:T(8,128)(2,1)S(1)}, u32[]{:S(2)}, u32[]{:S(2)}) collective-permute-start(bf16[2,384,256]{1,2,0:T(8,128)(2,1)S(1)} %collective-permute-done.1), channel_id=1, source_target_pairs={{0,2},{2,4},{4,6},{6,8},{8,10},{10,12},{12,14},{14,16},{16,18},{18... | collective-permute-start | bytes 1179656 | tf_op jit(solution)/shard_map/ppermute | solution.py:14
  36.0 9.1 %copy-start.7 = (bf16[2,384,256]{1,2,0:T(8,128)(2,1)}, bf16[2,384,256]{1,2,0:T(8,128)(2,1)S(1)}, u32[]{:S(2)}) copy-start(bf16[2,384,256]{1,2,0:T(8,128)(2,1)S(1)} %collective-permute-done.2) | copy-start | bytes 1179652
  36.1 9.1 %collective-permute-start.3 = (bf16[2,384,256]{1,2,0:T(8,128)(2,1)S(1)}, bf16[2,384,256]{1,2,0:T(8,128)(2,1)S(1)}, u32[]{:S(2)}, u32[]{:S(2)}) collective-permute-start(bf16[2,384,256]{1,2,0:T(8,128)(2,1)S(1)} %collective-permute-done.2), channel_id=1, source_target_pairs={{0,2},{2,4},{4,6},{6,8},{8,10},{10,12},{12,14},{14,16},{16,18},{18... | collective-permute-start | bytes 1179656 | tf_op jit(solution)/shard_map/ppermute | solution.py:14
  45.1 7.9 %copy-start.5 = (bf16[2,384,256]{1,2,0:T(8,128)(2,1)}, bf16[2,384,256]{1,2,0:T(8,128)(2,1)S(1)}, u32[]{:S(2)}) copy-start(bf16[2,384,256]{1,2,0:T(8,128)(2,1)S(1)} %collective-permute-done.3) | copy-start | bytes 1179652
  45.1 9.1 %collective-permute-start.4 = (bf16[2,384,256]{1,2,0:T(8,128)(2,1)S(1)}, bf16[2,384,256]{1,2,0:T(8,128)(2,1)S(1)}, u32[]{:S(2)}, u32[]{:S(2)}) collective-permute-start(bf16[2,384,256]{1,2,0:T(8,128)(2,1)S(1)} %collective-permute-done.3), channel_id=1, source_target_pairs={{0,2},{2,4},{4,6},{6,8},{8,10},{10,12},{12,14},{14,16},{16,18},{18... | collective-permute-start | bytes 1179656 | tf_op jit(solution)/shard_map/ppermute | solution.py:14
  54.2 26.1 %copy-start.4 = (bf16[2,384,256]{1,2,0:T(8,128)(2,1)}, bf16[2,384,256]{1,2,0:T(8,128)(2,1)S(1)}, u32[]{:S(2)}) copy-start(bf16[2,384,256]{1,2,0:T(8,128)(2,1)S(1)} %collective-permute-done.4) | copy-start | bytes 1179652
  54.2 9.1 %collective-permute-start.5 = (bf16[2,384,256]{1,2,0:T(8,128)(2,1)S(1)}, bf16[2,384,256]{1,2,0:T(8,128)(2,1)S(1)}, u32[]{:S(2)}, u32[]{:S(2)}) collective-permute-start(bf16[2,384,256]{1,2,0:T(8,128)(2,1)S(1)} %collective-permute-done.4), channel_id=1, source_target_pairs={{0,2},{2,4},{4,6},{6,8},{8,10},{10,12},{12,14},{14,16},{16,18},{18... | collective-permute-start | bytes 1179656 | tf_op jit(solution)/shard_map/ppermute | solution.py:14
  58.9 11.2 %copy-start.1 = (bf16[384,256]{1,0:T(8,128)(2,1)S(1)}, bf16[384,256]{1,0:T(8,128)(2,1)}, u32[]{:S(2)}) copy-start(bf16[384,256]{1,0:T(8,128)(2,1)} %param.23) | copy-start | bytes 589828
  59.9 9.0 %copy-start = (f32[2,384,384,4]{2,1,3,0:T(8,128)}, f32[2,384,384,4]{2,1,3,0:T(8,128)S(1)}, u32[]{:S(2)}) copy-start(f32[2,384,384,4]{2,1,3,0:T(8,128)S(1)} %get-tuple-element.445) | copy-start | bytes 14155780
  63.3 17.1 %copy-start.2 = (bf16[2,384,256]{1,2,0:T(8,128)(2,1)}, bf16[2,384,256]{1,2,0:T(8,128)(2,1)S(1)}, u32[]{:S(2)}) copy-start(bf16[2,384,256]{1,2,0:T(8,128)(2,1)S(1)} %collective-permute-done.5) | copy-start | bytes 1179652
  63.3 11.7 %collective-permute-start.6 = (bf16[2,384,256]{1,2,0:T(8,128)(2,1)S(1)}, bf16[2,384,256]{1,2,0:T(8,128)(2,1)}, u32[]{:S(2)}, u32[]{:S(2)}) collective-permute-start(bf16[2,384,256]{1,2,0:T(8,128)(2,1)S(1)} %collective-permute-done.5), channel_id=1, source_target_pairs={{0,2},{2,4},{4,6},{6,8},{8,10},{10,12},{12,14},{14,16},{16,18},{18... | collective-permute-start | bytes 1179656 | tf_op jit(solution)/shard_map/ppermute | solution.py:14
  75.1 21.0 %collective-permute-start.7 = (bf16[2,384,256]{1,2,0:T(8,128)(2,1)}, bf16[2,384,256]{1,2,0:T(8,128)(2,1)S(1)}, u32[]{:S(2)}, u32[]{:S(2)}) collective-permute-start(bf16[2,384,256]{1,2,0:T(8,128)(2,1)} %collective-permute-done.6), channel_id=1, source_target_pairs={{0,2},{2,4},{4,6},{6,8},{8,10},{10,12},{12,14},{14,16},{16,18},{18... | collective-permute-start | bytes 1179656 | tf_op jit(solution)/shard_map/ppermute | solution.py:14
  80.4 3.6 %copy-start.11 = (s32[3]{0:T(128)S(1)}, s32[3]{0:T(128)}, u32[]{:S(2)}) copy-start(s32[3]{0:T(128)} %param.24) | copy-start | bytes 40
  84.1 5.5 %copy-start.9 = (bf16[2,384,256]{1,2,0:T(8,128)(2,1)S(1)}, bf16[2,384,256]{1,2,0:T(8,128)(2,1)}, u32[]{:S(2)}) copy-start(bf16[2,384,256]{1,2,0:T(8,128)(2,1)} %copy-done.8) | copy-start | bytes 1179652
  94.1 1.0 copy-start.6
  95.1 1.0 copy-start.3
Sparse Core Ops, SparseCore 0:
  105.6 68.1 reduce-scatter.1
where the time goes:
time: 183 us; the launch traced here: 181 us
  waiting for transfers between devices  101 us (55%)
  starting transfers between devices  28 us (15%)
  matrix products  19 us (10%)
  between operations  18.6 us (10%)
  local copies, waits for them, and re-layouts  8.17 us (4%)
  other arithmetic  5.66 us (3%)
    reduce_scatter x1, waiting for transfers between devices, per_device(): lax.psum_scatter(lax.dot_general(out_weight, heads_out, (((0,), (1,)), ((...  68.3 us
    ppermute x8, waiting for transfers between devices, from_behind(): return lax.ppermute(block, axis, route)  32.3 us
    ppermute x8, starting transfers between devices, from_behind(): return lax.ppermute(block, axis, route)  28 us
    dot_general x1, matrix products, per_device(): lax.dot_general(out_weight, heads_out, (((0,), (1,)), ((), ())), preferre...  8.5 us
    dot_general x3, matrix products, attend(): jnp.einsum('gcpj,jgd->gcpd', expw.astype(jnp.bfloat16), val_blk, preferre...  7.66 us
    unnamed x27, local copies, waits for them, and re-layouts  5.5 us
  transfers between devices with their start and end apart: 9, of which 7 were waited for; matrix products, arithmetic and copies ran while one was open for 11% of the time, Pallas kernels for 0%

commit v1 on v0

v1 whole, which is shorter than its diff:
```python
import functools

import jax
import jax.numpy as jnp
from jax import lax
from jax.experimental import pallas as pl
from jax.experimental.pallas import tpu as pltpu
from jax.sharding import PartitionSpec as P

HEAD_SIZE = 128
BLOCK = 128
LOG2E = 1.4426950408889634
MASKED = -1e30


def shift(x, distance):
    n = lax.axis_size("ctx")
    return lax.ppermute(x, "ctx", [(i, i + distance) for i in range(n - distance)])


def swap(x, mask):
    return lax.ppermute(x, "ctx", [(i, i ^ mask) for i in range(lax.axis_size("ctx"))])


def split_scaled(q, factor):
    exact = q.astype(jnp.float32) * factor
    high = exact.astype(jnp.bfloat16)
    low = (exact - high.astype(jnp.float32)).astype(jnp.bfloat16)
    return jnp.concatenate([high, low], axis=1)


def attention_kernel(first, last, distances, n_head, starts_ref, recv_starts_ref, *refs):
    refs = list(refs)
    me = lax.axis_index("ctx")
    pair, core, col = me // 2, me % 2, (me // 2) % 2
    if first:
        queries_ref, q_recv_ref, own_ref = refs[:3]
        refs = refs[3:]
    else:
        q2_ref, top_in, acc_in = refs[:3]
        refs = refs[3:]
    pieces = refs[: len(distances)]
    refs = refs[len(distances) :]
    if first:
        q2_ref, top_ref, acc_ref = refs
    elif last:
        out_own, out_other, top_ref, acc_ref = refs
    else:
        top_ref, acc_ref = refs
    tok = starts_ref.shape[0] * BLOCK
    half = tok // BLOCK
    blocks = 2 * half
    rows = n_head * BLOCK

    def start_of(b):
        mine = b // half == core
        return jnp.where(mine, starts_ref[b % half], recv_starts_ref[b % half])

    def rows_of(ref, j, lane0):
        t = slice(j * BLOCK, (j + 1) * BLOCK)
        return jnp.concatenate(
            [ref[t, pl.ds(lane0 + h * HEAD_SIZE, HEAD_SIZE)] for h in range(n_head)], axis=0
        )

    def key_pair(piece_ref, width):
        k = piece_ref[:width, :HEAD_SIZE]
        return jnp.concatenate([k, k], axis=1)

    def value_ones(piece_ref, width):
        v = piece_ref[:width, HEAD_SIZE:]
        return jnp.concatenate([v, jnp.ones_like(v)], axis=1)

    def dot_t(a, b):
        return lax.dot_general(a, b, (((1,), (1,)), ((), ())), preferred_element_type=jnp.float32)

    if first:
        factor = HEAD_SIZE**-0.5 * LOG2E
        for j in range(half):
            mine = rows_of(queries_ref, j, pl.multiple_of(core * rows, rows))
            q2_ref[core * half + j] = split_scaled(mine, factor)
            other = rows_of(q_recv_ref, j, 0)
            q2_ref[(1 - core) * half + j] = split_scaled(other, factor)
        for b in range(blocks):
            width = (b + 1) * BLOCK
            s = dot_t(q2_ref[b], key_pair(own_ref, width))
            since = start_of(b) - pair * 2 * tok
            t_id = lax.broadcasted_iota(jnp.int32, (rows, BLOCK), 0) % BLOCK
            c_id = lax.broadcasted_iota(jnp.int32, (rows, BLOCK), 1)
            diag = jnp.where(c_id <= t_id, s[:, b * BLOCK :], MASKED)
            if b:
                k_id = lax.broadcasted_iota(jnp.int32, (rows, b * BLOCK), 1)
                s = jnp.concatenate([jnp.where(k_id >= since, s[:, : b * BLOCK], MASKED), diag], 1)
            else:
                s = diag
            top = jnp.max(s, axis=1, keepdims=True)
            p = jnp.exp2(s - top).astype(jnp.bfloat16)
            top_ref[b] = jnp.broadcast_to(top, (rows, HEAD_SIZE))
            acc_ref[b] = jnp.dot(p, value_ones(own_ref, width), preferred_element_type=jnp.float32)
    else:
        top_ref[...] = top_in[...]
        acc_ref[...] = acc_in[...]

    def update(b, piece_ref, since):
        s = dot_t(q2_ref[b], key_pair(piece_ref, 2 * tok))
        if since is not None:
            k_id = lax.broadcasted_iota(jnp.int32, s.shape, 1)
            s = jnp.where(k_id >= since, s, MASKED)
        old = top_ref[b][:, :1]
        top = jnp.maximum(old, jnp.max(s, axis=1, keepdims=True))
        p = jnp.exp2(s - top).astype(jnp.bfloat16)
        top_ref[b] = jnp.broadcast_to(top, (rows, HEAD_SIZE))
        acc_ref[b] = acc_ref[b] * jnp.exp2(old - top) + jnp.dot(
            p, value_ones(piece_ref, 2 * tok), preferred_element_type=jnp.float32
        )

    for (if_left, if_right), piece_ref in zip(distances, pieces, strict=True):
        base = (pair - jnp.where(col == 0, if_left, if_right)) * 2 * tok
        whole = start_of(blocks - 1) <= base

        @pl.when(whole)
        def _(piece_ref=piece_ref):
            @pl.loop(0, blocks)
            def _(b):
                update(b, piece_ref, None)

        @pl.when(jnp.logical_not(whole))
        def _(piece_ref=piece_ref, base=base):
            @pl.loop(0, blocks)
            def _(b):
                since = start_of(b) - base

                @pl.when(since < 2 * tok)
                def _():
                    update(b, piece_ref, since)

    if last:
        for j in range(half):
            for out, shard in ((out_own, core), (out_other, 1 - core)):
                acc = acc_ref[shard * half + j]
                o = (acc[:, :HEAD_SIZE] / acc[:, HEAD_SIZE:]).astype(jnp.bfloat16)
                for h in range(n_head):
                    out[j * BLOCK : (j + 1) * BLOCK, h * HEAD_SIZE : (h + 1) * HEAD_SIZE] = o[
                        h * BLOCK : (h + 1) * BLOCK
                    ]


def attention_call(first, last, distances, n_head, starts, recv_starts, operands):
    tok = starts.shape[0] * BLOCK
    blocks, rows = 2 * starts.shape[0], n_head * BLOCK
    state = [
        jax.ShapeDtypeStruct((blocks, rows, HEAD_SIZE), jnp.float32),
        jax.ShapeDtypeStruct((blocks, rows, 2 * HEAD_SIZE), jnp.float32),
    ]
    scratch = []
    if first:
        outs = [jax.ShapeDtypeStruct((blocks, rows, 2 * HEAD_SIZE), jnp.bfloat16)] + state
    elif last:
        outs = [jax.ShapeDtypeStruct((tok, rows), jnp.bfloat16)] * 2
        scratch = [pltpu.VMEM(s.shape, s.dtype) for s in state]
    else:
        outs = state
    n_pieces = len(distances) + 0.5 * first
    vmem, smem = pl.BlockSpec(memory_space=pltpu.VMEM), pl.BlockSpec(memory_space=pltpu.SMEM)
    return pl.pallas_call(
        functools.partial(attention_kernel, first, last, distances, n_head),
        out_shape=outs,
        in_specs=[smem, smem] + [vmem] * len(operands),
        out_specs=[vmem] * len(outs),
        scratch_shapes=scratch,
        compiler_params=pltpu.CompilerParams(vmem_limit_bytes=40 * 2**20),
        cost_estimate=pl.CostEstimate(
            flops=int(n_pieces * blocks * rows * 2 * tok * HEAD_SIZE * 8),
            bytes_accessed=8 * 2**20,
            transcendentals=int(n_pieces * blocks * rows * 2 * tok),
        ),
    )(starts, recv_starts, *operands)


def per_device(queries, keys, values, block_start, out_weight):
    tok = queries.shape[0]
    group = queries.shape[1] // 2
    n_head = group // HEAD_SIZE
    me = lax.axis_index("ctx")
    core, col = me % 2, (me // 2) % 2
    head = lax.axis_index("head")

    def part(x, index, size):
        return lax.dynamic_slice_in_dim(x, index * size, size, 1)

    mine = jnp.concatenate([part(keys, core, HEAD_SIZE), part(values, core, HEAD_SIZE)], 1)
    theirs = jnp.concatenate([part(keys, 1 - core, HEAD_SIZE), part(values, 1 - core, HEAD_SIZE)], 1)
    recv = swap(theirs, 1)
    own = jnp.where(core == 0, jnp.concatenate([mine, recv]), jnp.concatenate([recv, mine]))
    one_behind = shift(own, 4)
    q_recv = swap(part(queries, 1 - core, group), 1)
    recv_starts = swap(block_start, 1)
    two_behind = shift(one_behind, 4)
    across = swap(one_behind, 2)
    q2, top, acc = attention_call(
        True, False, ((2, 2),), n_head, block_start, recv_starts, (queries, q_recv, own, one_behind)
    )
    third = swap(jnp.where(col == 1, two_behind, own), 2)
    top, acc = attention_call(
        False, False, ((1, 3), (4, 4)), n_head, block_start, recv_starts,
        (q2, top, acc, across, two_behind),
    )
    o_own, o_other = attention_call(
        False, True, ((3, 1),), n_head, block_start, recv_starts, (q2, top, acc, third)
    )
    o_recv = swap(o_other, 1)
    heads_out = jnp.where(
        core == 0, jnp.concatenate([o_own, o_recv], 1), jnp.concatenate([o_recv, o_own], 1)
    )
    cols = out_weight.shape[1] // 2
    away = jnp.dot(heads_out, part(out_weight, 1 - head, cols), preferred_element_type=jnp.float32)
    away = lax.ppermute(away.astype(jnp.bfloat16), "head", [(0, 1), (1, 0)])
    here = jnp.dot(heads_out, part(out_weight, head, cols), preferred_element_type=jnp.float32)
    here = here.astype(jnp.bfloat16).astype(jnp.float32)
    return (here + away.astype(jnp.float32)).astype(jnp.bfloat16)


def solution(mesh):
    in_specs = (P("ctx", "head"), P("ctx", "head"), P("ctx", "head"), P("ctx"), P("head", None))
    out_specs = P("ctx", "head")
    return jax.shard_map(
        per_device, mesh=mesh, in_specs=in_specs, out_specs=out_specs, check_vma=False
    )
```

time: 183 us -> 100 us (0.55)
  the two profiles are of different devices: /device:TPU:2 before, /device:TPU:14 now
where the time goes in v1:
time: 100 us
  waiting for transfers between devices  45.2 us (45%)
  Pallas kernels  33.1 us (33%)
  starting transfers between devices  9.42 us (9%)
  matrix products  9.16 us (9%)
  other arithmetic  1.99 us (2%)
  local copies, waits for them, and re-layouts  1.18 us (1%)
    pallas_call x3, Pallas kernels, attention_call(): pl.pallas_call(functools.partial(attention_kernel, first, last, distances...  33.1 us
    ppermute x1, waiting for transfers between devices, per_device(): away = lax.ppermute(away.astype(jnp.bfloat16), 'head', [(0, 1), (1, 0)])  32.1 us
    ppermute x2, waiting for transfers between devices, shift(): lax.ppermute(x, 'ctx', [(i, i + distance) for i in range(n - distance)])  9.43 us
    ppermute x2, starting transfers between devices, shift(): lax.ppermute(x, 'ctx', [(i, i + distance) for i in range(n - distance)])  6.96 us
    dot_general x1, matrix products, per_device(): jnp.dot(heads_out, part(out_weight, 1 - head, cols), preferred_element_ty...  5.15 us
    dot_general x1, matrix products, per_device(): jnp.dot(heads_out, part(out_weight, head, cols), preferred_element_type=j...  4.01 us
    ppermute x6, waiting for transfers between devices, swap(): lax.ppermute(x, 'ctx', [(i, i ^ mask) for i in range(lax.axis_size('ctx'))])  3.67 us
  transfers between devices with their start and end apart: 9, of which 6 were waited for; matrix products, arithmetic and copies ran while one was open for 4% of the time, Pallas kernels for 23%

profile of v1, /device:TPU:14, one launch (start us, length us, event | category | flops | bytes accessed | tf_op | source)
XLA Modules:
  0.0 100.2 jit_solution(428299366855582960)
XLA Ops:
  0.0 0.0 copy-start
  0.0 0.0 copy-start.1
  0.0 1.1 %constant_dynamic-slice_fusion.2 = (bf16[384,128]{1,0:T(8,128)(2,1)S(1)}, bf16[384,128]{1,0:T(8,128)(2,1)S(1)}, bf16[384,128]{1,0:T(8,128)(2,1)S(1)}, bf16[384,128]{1,0:T(8,128)(2,1)S(1)}) fusion(bf16[384,256]{1,0:T(8,128)(2,1)} %param.7, s32[]{:T(128)S(6)} %select_n.58, s32[]{:T(128)S(6)} %select_n.59, bf16[384,256]{1,0:T(8,128)(2,1)} %param.6), kind=kLoop, calls=%fused_computation.15 | loop fusion | bytes 786440 | tf_op jit(solution)/shard_map/dynamic_slice | solution.py:188
  1.2 0.1 collective-permute-start.2
  1.3 1.4 %collective-permute-done.2 = bf16[384,256]{1,0:T(8,128)(2,1)S(1)} collective-permute-done((bf16[384,256]{1,0:T(8,128)(2,1)S(1)}, bf16[384,256]{1,0:T(8,128)(2,1)S(1)}, u32[]{:S(2)}, u32[]{:S(2)}) %collective-permute-start.2) | collective-permute-done | bytes 196640 | tf_op jit(solution)/shard_map/ppermute | solution.py:22
  2.7 0.2 maximum_select_fusion.1.refs_2_
  2.9 3.5 %collective-permute-start.3 = (bf16[768,256]{1,0:T(8,128)(2,1)S(1)}, bf16[768,256]{1,0:T(8,128)(2,1)S(1)}, u32[]{:S(2)}, u32[]{:S(2)}) collective-permute-start(bf16[768,256]{1,0:T(8,128)(2,1)S(1)} %maximum_select_fusion.1.refs_2_), channel_id=1, source_target_pairs={{0,8},{2,10},{4,12},{6,14},{8,16},{10,18},{12,20},{14,22},{16,24},... | collective-permute-start | bytes 1179656 | tf_op jit(solution)/shard_map/ppermute | solution.py:18
  6.3 0.0 copy-done
  6.4 0.1 collective-permute-start.1
  6.5 9.4 %collective-permute-done.3.refs_3_ = bf16[768,256]{1,0:T(8,128)(2,1)S(1)} collective-permute-done((bf16[768,256]{1,0:T(8,128)(2,1)S(1)}, bf16[768,256]{1,0:T(8,128)(2,1)S(1)}, u32[]{:S(2)}, u32[]{:S(2)}) %collective-permute-start.3) | collective-permute-done | bytes 393248 | tf_op jit(solution)/shard_map/ppermute | solution.py:18
  15.9 3.5 %collective-permute-start.5 = (bf16[768,256]{1,0:T(8,128)(2,1)S(1)}, bf16[768,256]{1,0:T(8,128)(2,1)S(1)}, u32[]{:S(2)}, u32[]{:S(2)}) collective-permute-start(bf16[768,256]{1,0:T(8,128)(2,1)S(1)} %collective-permute-done.3.refs_3_), channel_id=1, source_target_pairs={{0,8},{2,10},{4,12},{6,14},{8,16},{10,18},{12,20},{14,22},{16,24},... | collective-permute-start | bytes 1179656 | tf_op jit(solution)/shard_map/ppermute | solution.py:18
  19.4 0.0 copy-done.1
  19.4 0.1 collective-permute-start
  19.5 0.6 collective-permute-start.4
  20.1 0.5 collective-permute-done.recv_starts_ref
  20.6 0.0 collective-permute-done.1.refs_1_
  20.6 12.5 %shard_map.55 = (bf16[6,512,256]{2,1,0:T(8,128)(2,1)S(1)}, f32[6,512,128]{2,1,0:T(8,128)S(1)}, f32[6,512,256]{2,1,0:T(8,128)S(1)}) custom-call(s32[3]{0:T(128)S(1)} %copy-done.1, s32[3]{0:T(128)S(1)} %collective-permute-done.recv_starts_ref, bf16[384,1024]{1,0:T(8,128)(2,1)S(1)} %copy-done, bf16[384,512]{1,0:T(8,128)(2,1)S(1)} %collective-permute-done.1.refs_1_, ...), custom_call_target="tpu_custom_call" | custom-call | flops 3623878656 | bytes 8388608 | tf_op jit(solution)/shard_map/pallas_call | solution.py:164
  33.1 0.0 collective-permute-done.5.refs_4_
  33.2 1.1 %collective-permute-start.6 = (bf16[768,256]{1,0:T(8,128)(2,1)S(1)}, bf16[768,256]{1,0:T(8,128)(2,1)S(1)}, u32[]{:S(2)}, u32[]{:S(2)}) collective-permute-start(bf16[768,256]{1,0:T(8,128)(2,1)S(1)} %broadcast_select_fusion), channel_id=1, source_target_pairs={{0,4},{2,6},{4,0},{6,2},{8,12},{10,14},{12,8},{14,10},{16,20},{18,... | collective-permute-start | bytes 1179656 | tf_op jit(solution)/shard_map/ppermute | solution.py:22
  34.3 0.0 collective-permute-done.4.refs_3_
  34.3 10.1 %shard_map.56 = (f32[6,512,128]{2,1,0:T(8,128)S(1)}, f32[6,512,256]{2,1,0:T(8,128)S(1)}) custom-call(s32[3]{0:T(128)S(1)} %copy-done.1, s32[3]{0:T(128)S(1)} %collective-permute-done.recv_starts_ref, bf16[6,512,256]{2,1,0:T(8,128)(2,1)S(1)} %get-tuple-element.12.refs_0_, f32[6,512,128]{2,1,0:T(8,128)S(1)} %get-tuple-element.13.refs_1_, ...), custom_call_target="tpu_custom_call" | custom-call | flops 4831838208 | bytes 8388608 | tf_op jit(solution)/shard_map/pallas_call | solution.py:164
  44.4 0.1 collective-permute-done.6.refs_3_
  44.5 10.4 %shard_map.57 = (bf16[384,512]{1,0:T(8,128)(2,1)S(1)}, bf16[384,512]{1,0:T(8,128)(2,1)S(1)}) custom-call(s32[3]{0:T(128)S(1)} %copy-done.1, s32[3]{0:T(128)S(1)} %collective-permute-done.recv_starts_ref, bf16[6,512,256]{2,1,0:T(8,128)(2,1)S(1)} %get-tuple-element.12.refs_0_, f32[6,512,128]{2,1,0:T(8,128)S(1)} %get-tuple-element.15.refs_1_, ...), custom_call_target="tpu_custom_call" | custom-call | flops 2415919104 | bytes 8388608 | tf_op jit(solution)/shard_map/pallas_call | solution.py:164
  54.9 0.1 collective-permute-start.7
  55.0 1.7 %collective-permute-done.7 = bf16[384,512]{1,0:T(8,128)(2,1)S(1)} collective-permute-done((bf16[384,512]{1,0:T(8,128)(2,1)S(1)}, bf16[384,512]{1,0:T(8,128)(2,1)S(1)}, u32[]{:S(2)}, u32[]{:S(2)}) %collective-permute-start.7) | collective-permute-done | bytes 393248 | tf_op jit(solution)/shard_map/ppermute | solution.py:22
  56.7 5.2 %fusion.7 = bf16[384,2048]{1,0:T(8,128)(2,1)} fusion(bf16[1024,4096]{1,0:T(8,128)(2,1)} %param.9, s32[]{:T(128)S(6)} %select_n.67, bf16[384,512]{1,0:T(8,128)(2,1)S(1)} %collective-permute-done.7, bf16[384,512]{1,0:T(8,128)(2,1)S(1)} %get-tuple-element.17, pred[]{:T(512)S(6)} %eq.10), kind=kOutput, calls=%fused_computation.6 | convolution fusion | flops 1614938112 | bytes 6553605 | tf_op jit(solution)/shard_map/dot_general | solution.py:215
  61.9 0.5 collective-permute-start.8
  62.3 4.0 %fusion.4 = bf16[384,2048]{1,0:T(8,128)(2,1)S(1)} fusion(bf16[1024,4096]{1,0:T(8,128)(2,1)} %param.9, s32[]{:T(128)S(6)} %select_n.66, bf16[384,512]{1,0:T(8,128)(2,1)S(1)} %collective-permute-done.7, bf16[384,512]{1,0:T(8,128)(2,1)S(1)} %get-tuple-element.17, pred[]{:T(512)S(6)} %eq.10), kind=kOutput, calls=%fused_computation.5 | convolution fusion | flops 1614938112 | bytes 6553605 | tf_op jit(solution)/shard_map/dot_general | solution.py:217
  66.4 32.1 %collective-permute-done.8 = bf16[384,2048]{1,0:T(8,128)(2,1)S(1)} collective-permute-done((bf16[384,2048]{1,0:T(8,128)(2,1)}, bf16[384,2048]{1,0:T(8,128)(2,1)S(1)}, u32[]{:S(2)}, u32[]{:S(2)}) %collective-permute-start.8) | collective-permute-done | bytes 1572896 | tf_op jit(solution)/shard_map/ppermute | solution.py:216
  98.5 1.8 %add_convert_fusion = bf16[384,2048]{1,0:T(8,128)(2,1)} fusion(bf16[384,2048]{1,0:T(8,128)(2,1)S(1)} %collective-permute-done.8, bf16[384,2048]{1,0:T(8,128)(2,1)S(1)} %fusion.4), kind=kLoop, calls=%fused_computation.4 | loop fusion | flops 3145728 | bytes 4718592 | tf_op jit(solution)/shard_map/convert_element_type | solution.py:219
  (3 shorter events, 0.1 us)
Async XLA Ops:
  0.0 6.3 %copy-start = (bf16[384,1024]{1,0:T(8,128)(2,1)S(1)}, bf16[384,1024]{1,0:T(8,128)(2,1)}, u32[]{:S(2)}) copy-start(bf16[384,1024]{1,0:T(8,128)(2,1)} %refs_0_.1) | copy-start | bytes 2359300
  0.0 19.4 %copy-start.1 = (s32[3]{0:T(128)S(1)}, s32[3]{0:T(128)}, u32[]{:S(2)}) copy-start(s32[3]{0:T(128)} %starts_ref.5) | copy-start | bytes 40
  1.2 1.5 %collective-permute-start.2 = (bf16[384,256]{1,0:T(8,128)(2,1)S(1)}, bf16[384,256]{1,0:T(8,128)(2,1)S(1)}, u32[]{:S(2)}, u32[]{:S(2)}) collective-permute-start(bf16[384,256]{1,0:T(8,128)(2,1)S(1)} %pad_maximum_fusion), channel_id=1, source_target_pairs={{0,2},{2,0},{4,6},{6,4},{8,10},{10,8},{12,14},{14,12},{16,18},{18,... | collective-permute-start | bytes 589832 | tf_op jit(solution)/shard_map/ppermute | solution.py:22
  2.9 13.1 %collective-permute-start.3 = (bf16[768,256]{1,0:T(8,128)(2,1)S(1)}, bf16[768,256]{1,0:T(8,128)(2,1)S(1)}, u32[]{:S(2)}, u32[]{:S(2)}) collective-permute-start(bf16[768,256]{1,0:T(8,128)(2,1)S(1)} %maximum_select_fusion.1.refs_2_), channel_id=1, source_target_pairs={{0,8},{2,10},{4,12},{6,14},{8,16},{10,18},{12,20},{14,22},{16,24},... | collective-permute-start | bytes 1179656 | tf_op jit(solution)/shard_map/ppermute | solution.py:18
  6.4 14.2 %collective-permute-start.1 = (bf16[384,512]{1,0:T(8,128)(2,1)S(1)}, bf16[384,512]{1,0:T(8,128)(2,1)S(1)}, u32[]{:S(2)}, u32[]{:S(2)}) collective-permute-start(bf16[384,512]{1,0:T(8,128)(2,1)S(1)} %constant_dynamic-slice_fusion.4), channel_id=1, source_target_pairs={{0,2},{2,0},{4,6},{6,4},{8,10},{10,8},{12,14},{14,12},{16,18},{18,... | collective-permute-start | bytes 1179656 | tf_op jit(solution)/shard_map/ppermute | solution.py:22
  15.9 17.2 %collective-permute-start.5 = (bf16[768,256]{1,0:T(8,128)(2,1)S(1)}, bf16[768,256]{1,0:T(8,128)(2,1)S(1)}, u32[]{:S(2)}, u32[]{:S(2)}) collective-permute-start(bf16[768,256]{1,0:T(8,128)(2,1)S(1)} %collective-permute-done.3.refs_3_), channel_id=1, source_target_pairs={{0,8},{2,10},{4,12},{6,14},{8,16},{10,18},{12,20},{14,22},{16,24},... | collective-permute-start | bytes 1179656 | tf_op jit(solution)/shard_map/ppermute | solution.py:18
  19.4 1.2 %collective-permute-start = (s32[3]{0:T(128)S(1)}, s32[3]{0:T(128)S(1)}, u32[]{:S(2)}, u32[]{:S(2)}) collective-permute-start(s32[3]{0:T(128)S(1)} %copy-done.1), channel_id=1, source_target_pairs={{0,2},{2,0},{4,6},{6,4},{8,10},{10,8},{12,14},{14,12},{16,18},{18,... | collective-permute-start | bytes 44 | tf_op jit(solution)/shard_map/ppermute | solution.py:22
  19.5 14.8 %collective-permute-start.4 = (bf16[768,256]{1,0:T(8,128)(2,1)S(1)}, bf16[768,256]{1,0:T(8,128)(2,1)S(1)}, u32[]{:S(2)}, u32[]{:S(2)}) collective-permute-start(bf16[768,256]{1,0:T(8,128)(2,1)S(1)} %collective-permute-done.3.refs_3_), channel_id=1, source_target_pairs={{0,4},{2,6},{4,0},{6,2},{8,12},{10,14},{12,8},{14,10},{16,20},{18,... | collective-permute-start | bytes 1179656 | tf_op jit(solution)/shard_map/ppermute | solution.py:22
  33.2 11.3 %collective-permute-start.6 = (bf16[768,256]{1,0:T(8,128)(2,1)S(1)}, bf16[768,256]{1,0:T(8,128)(2,1)S(1)}, u32[]{:S(2)}, u32[]{:S(2)}) collective-permute-start(bf16[768,256]{1,0:T(8,128)(2,1)S(1)} %broadcast_select_fusion), channel_id=1, source_target_pairs={{0,4},{2,6},{4,0},{6,2},{8,12},{10,14},{12,8},{14,10},{16,20},{18,... | collective-permute-start | bytes 1179656 | tf_op jit(solution)/shard_map/ppermute | solution.py:22
  54.9 1.8 %collective-permute-start.7 = (bf16[384,512]{1,0:T(8,128)(2,1)S(1)}, bf16[384,512]{1,0:T(8,128)(2,1)S(1)}, u32[]{:S(2)}, u32[]{:S(2)}) collective-permute-start(bf16[384,512]{1,0:T(8,128)(2,1)S(1)} %get-tuple-element.18), channel_id=1, source_target_pairs={{0,2},{2,0},{4,6},{6,4},{8,10},{10,8},{12,14},{14,12},{16,18},{18,... | collective-permute-start | bytes 1179656 | tf_op jit(solution)/shard_map/ppermute | solution.py:22
  61.9 36.6 %collective-permute-start.8 = (bf16[384,2048]{1,0:T(8,128)(2,1)}, bf16[384,2048]{1,0:T(8,128)(2,1)S(1)}, u32[]{:S(2)}, u32[]{:S(2)}) collective-permute-start(bf16[384,2048]{1,0:T(8,128)(2,1)} %fusion.7), channel_id=1, source_target_pairs={{0,1},{1,0},{2,3},{3,2},{4,5},{5,4},{6,7},{7,6},{8,9},{9,8},{10,11... | collective-permute-start | bytes 4718600 | tf_op jit(solution)/shard_map/ppermute | solution.py:216
